TPU v7x, 32 devices: a whole 2x2x4 slice. The times are simulated.
32 devices in a mesh: groups: 2 (over x), row: 16 (over z, y, core).
Axes of the slice: x: 2, y: 2, z: 4, core: 2. Of those that a mesh axis runs over, the one named last changes fastest.
Arguments:
- amplitudes: float32 [6144, 16384], P('row', 'groups'), parts along dimension 1, may hold values from -6 to 6
- integrals: float32 [6144, 1024], P('row', 'groups'), parts along dimension 1, may hold values from -0.21875 to 0.21875
- pair_irrep: int32 [192], P('groups'), parts along dimension 0, may hold values from 0 to 7
- column_irrep: int32 [16], P('groups'), parts along dimension 0, may hold values from 0 to 7
Outputs:
- cycle_term: float32 [8192, 1024], P('row', 'groups'), parts along dimension 1
There are 2 independent parts, one for each index of `groups`. A program takes and returns all parts, laid end to end along the dimension named above; each array names one. Nothing has to cross between parts.
All inputs are finite; a program needn't handle non-finite values.
Results may differ from a plain program's by a relative error of at most 0.000075.
Values sent between devices are 32-bit elements; how exact they have to be, the bound alone decides.
A program may use at most 128 MiB of HBM per device.

v0:
```python
import jax
import jax.numpy as jnp
from jax import lax
from jax.sharding import PartitionSpec as P

TILE = 64


def shards(amplitudes, integrals, pair_irrep, column_irrep):
    local_k = integrals.shape[0]
    row_labels = jnp.broadcast_to(pair_irrep[:, None], (pair_irrep.shape[0], TILE)).reshape(-1)
    col_labels = jnp.broadcast_to(column_irrep[:, None], (column_irrep.shape[0], TILE)).reshape(-1)
    offset = lax.axis_index("row") * local_k
    labels = lax.dynamic_slice_in_dim(row_labels, offset, integrals.shape[0], 0)
    masked = jnp.where(labels[:, None] == col_labels[None, :], integrals, jnp.zeros_like(integrals))
    return lax.psum_scatter(
        lax.dot_general(
            amplitudes,
            masked,
            (((0,), (0,)), ((), ())),
            precision=lax.Precision.HIGHEST,
            preferred_element_type=jnp.float32,
        ),
        "row",
        scatter_dimension=0,
        tiled=True,
    )


def solution(mesh):
    placed = (P("row", "groups"), P("row", "groups"), P("groups"), P("groups"))
    return jax.shard_map(
        shards, mesh=mesh, in_specs=placed, out_specs=P("row", "groups"), check_vma=False
    )
```

profile of v0, /device:TPU:25, one launch (start us, length us, event | category | flops | bytes accessed | tf_op | source)
XLA Modules:
  0.0 227.3 jit_solution(129871606872154054)
XLA Ops:
  6.5 0.0 reduce-scatter.2.cloned.1.call-start
  6.5 0.7 broadcast_in_dim.7
  7.3 0.1 eq.16
  7.3 0.7 broadcast_in_dim.6
  8.1 0.1 reshape.7
  8.1 0.1 dynamic_slice.3
  8.2 31.6 %convolution_bitcast_fusion = f32[8192,512]{0,1:T(8,128)} fusion(f32[384,8192]{1,0:T(8,128)} %param.4, f32[384,512]{1,0:T(8,128)} %param.5, s32[512]{0:T(512)S(1)} %eq.16, s32[384]{0:T(512)S(1)} %dynamic_slice.3), kind=kOutput, calls=%fused_computation | convolution fusion | flops 19327746048 | bytes 30150144 | tf_op jit(solution)/shard_map/dot_general | solution.py:17
  39.8 0.0 reduce-scatter.2.cloned.1.call-update
  39.9 178.1 %reduce-scatter.2.cloned.1.call-done = f32[512,512]{0,1:T(8,128)} async-done(((f32[8192,512]{0,1:T(8,128)}), f32[512,512]{0,1:T(8,128)}) %reduce-scatter.2.cloned.1.call-update) | async-done | bytes 1048592 | tf_op jit(solution)/shard_map/reduce_scatter | solution.py:16
  217.9 2.5 %copy.6 = f32[512,512]{1,0:T(8,128)} copy(f32[512,512]{0,1:T(8,128)} %reduce-scatter.2.cloned.1.call-done) | data formatting | bytes 2097152 | tf_op jit(solution)/shard_map/reduce_scatter | solution.py:16
Async XLA Ops:
  6.5 211.4 %reduce-scatter.2.cloned.1.call-start = ((), (), s32[]{:S(2)}) async-start(), calls=%async_computation.1 | async-start | bytes 17825792 | tf_op jit(solution)/shard_map/reduce_scatter | solution.py:16
Sparse Core Ops, SparseCore 0:
  40.0 177.9 reduce-scatter.1
where the time goes:
time: 231 us; the launch traced here: 227 us
  waiting for transfers between devices  178 us (77%)
  matrix products  31.6 us (14%)
  between operations  13.4 us (6%)
  local copies, waits for them, and re-layouts  4.21 us (2%)
    reduce_scatter x1, waiting for transfers between devices, shards(): lax.psum_scatter(lax.dot_general(amplitudes, masked, (((0,), (0,)), ((),...  178 us
    dot_general x1, matrix products, shards(): lax.dot_general(amplitudes, masked, (((0,), (0,)), ((), ())), precision=l...  31.6 us
  transfers between devices with their start and end apart: 1, of which 1 were waited for; matrix products, arithmetic and copies ran while one was open for 0% of the time, Pallas kernels for 0%

commit v1 on v0

v1 whole, which is shorter than its diff:
```python
import functools

import jax
import jax.numpy as jnp
from jax import lax
from jax.experimental import pallas as pl
from jax.experimental.pallas import tpu as pltpu
from jax.sharding import PartitionSpec as P

TILE = 64
MESH = pl.DeviceIdType.MESH
CHUNKS = 4


def split(x):
    high = x.astype(jnp.bfloat16)
    low = (x - high.astype(jnp.float32)).astype(jnp.bfloat16)
    return high, low


def kernel(depth, a_hbm, b_hbm, pair_ref, column_ref, out_ref, a_buf, b_buf, b_high, b_low, part, from_y, from_z,
           a_sem, b_sem, a_send, a_recv, b_send, b_recv, y_send, y_recv, z_send, z_recv):
    local_k, width = b_hbm.shape
    rows = out_ref.shape[0]
    chunk = rows // CHUNKS
    me = lax.axis_index("row")
    z, y, c = me // 4, (me // 2) % 2, me % 2
    sibling = me + 1 - 2 * c
    across = me + 2 - 4 * y
    up, down = z < depth - 1, z > 0

    order = []
    low, high = z * 0, z * 0 + depth - 1
    for _ in range(depth):
        take_high = (high - z) > (z - low)
        order.append(jnp.where(take_high, high, low))
        low, high = jnp.where(take_high, low, low + 1), jnp.where(take_high, high - 1, high)

    def layer(s):
        found = order[0]
        for k in range(1, depth):
            found = jnp.where(s == k, order[k], found)
        return found

    def columns(b, core):
        other = 1 - b // depth
        side = y + other * (1 - 2 * y)
        owner = 4 * layer(b % depth) + 2 * side + core
        return pl.ds(pl.multiple_of(owner * rows, rows), rows)

    def a_local(b):
        return pltpu.make_async_copy(a_hbm.at[:, columns(b, c)], a_buf.at[b, pl.ds(0, local_k)], a_sem.at[b])

    def a_swap(b):
        return pltpu.make_async_remote_copy(
            src_ref=a_hbm.at[:, columns(b, 1 - c)], dst_ref=a_buf.at[b, pl.ds(local_k, local_k)],
            send_sem=a_send.at[b], recv_sem=a_recv.at[b], device_id={"row": sibling}, device_id_type=MESH)

    b_local = pltpu.make_async_copy(b_hbm, b_buf.at[pl.ds(0, local_k)], b_sem)
    b_swap = pltpu.make_async_remote_copy(
        src_ref=b_hbm, dst_ref=b_buf.at[pl.ds(local_k, local_k)], send_sem=b_send, recv_sem=b_recv,
        device_id={"row": sibling}, device_id_type=MESH)

    def y_copy(s, q):
        span = pl.ds(q * chunk, chunk)
        return pltpu.make_async_remote_copy(
            src_ref=part.at[s, span], dst_ref=from_y.at[s, span], send_sem=y_send.at[s, q], recv_sem=y_recv.at[s, q],
            device_id={"row": across}, device_id_type=MESH)

    def z_copy(s, q):
        target = layer(s)
        step = jnp.where(target > z, 1, -1)
        arrives_from_above = (target < z) & (z - 1 == target)
        slot = jnp.where(arrives_from_above, depth, target)
        span = pl.ds(q * chunk, chunk)
        return pltpu.make_async_remote_copy(
            src_ref=part.at[depth + s, span], dst_ref=from_z.at[slot, span], send_sem=z_send.at[s, q],
            recv_sem=z_recv.at[slot, q], device_id={"row": me + 4 * step}, device_id_type=MESH)

    def z_arrival(slot, q):
        span = pl.ds(q * chunk, chunk)
        return pltpu.make_async_remote_copy(
            src_ref=from_z.at[slot, span], dst_ref=from_z.at[slot, span], send_sem=z_send.at[0, q],
            recv_sem=z_recv.at[slot, q], device_id={"row": across}, device_id_type=MESH)

    b_local.start()
    for b in range(2 * depth):
        a_local(b).start()

    barrier = pltpu.get_barrier_semaphore()
    pl.semaphore_signal(barrier, inc=1, device_id={"row": sibling}, device_id_type=MESH)
    pl.semaphore_signal(barrier, inc=1, device_id={"row": across}, device_id_type=MESH)

    @pl.when(up)
    def _():
        pl.semaphore_signal(barrier, inc=1, device_id={"row": me + 4}, device_id_type=MESH)

    @pl.when(down)
    def _():
        pl.semaphore_signal(barrier, inc=1, device_id={"row": me - 4}, device_id_type=MESH)

    pl.semaphore_wait(barrier, 2 + jnp.where(up, 1, 0) + jnp.where(down, 1, 0))

    b_swap.start()
    for b in range(2 * depth):
        a_swap(b).start()

    block_of = lax.broadcasted_iota(jnp.int32, (TILE, width), 1) // TILE
    labels = jnp.zeros((TILE, width), jnp.int32)
    for j in range(width // TILE):
        labels = jnp.where(block_of == j, column_ref[j], labels)

    def mask(i, owner, base):
        span = pl.ds(pl.multiple_of(base + i * TILE, TILE), TILE)
        label = pair_ref[owner * (local_k // TILE) + i]
        kept = jnp.where(labels == label, b_buf[span, :], 0.0)
        b_high[span, :], b_low[span, :] = split(kept)

    b_local.wait()
    for i in range(local_k // TILE):
        mask(i, me, 0)
    b_swap.wait_recv()
    for i in range(local_k // TILE):
        mask(i, sibling, local_k)

    half = rows // 2

    def multiply(b, _):
        a_local(b).wait()
        a_swap(b).wait_recv()
        for t in range(2):
            high, low = split(a_buf[b, :, pl.ds(t * half, half)].T)
            dot = functools.partial(jnp.dot, preferred_element_type=jnp.float32)
            part[b, pl.ds(t * half, half), :] = (
                dot(high, b_high[...]) + dot(high, b_low[...]) + dot(low, b_high[...]))

            @pl.when(b < depth)
            def _():
                for q in range(t * CHUNKS // 2, (t + 1) * CHUNKS // 2):
                    y_copy(b, q).start()
        return 0

    lax.fori_loop(0, 2 * depth, multiply, 0)

    def forward(s, _):
        target = layer(s)
        fed = ((target > z) & down) | ((target < z) & up)
        for q in range(CHUNKS):
            span = pl.ds(q * chunk, chunk)
            y_copy(s, q).wait_recv()
            part[depth + s, span, :] += from_y[s, span, :]

            @pl.when(fed)
            def _():
                z_arrival(target, q).wait_recv()
                part[depth + s, span, :] += from_z[target, span, :]

            z_copy(s, q).start()
        return 0

    lax.fori_loop(0, depth - 1, forward, 0)

    last = depth - 1
    for q in range(CHUNKS):
        span = pl.ds(q * chunk, chunk)
        y_copy(last, q).wait_recv()
        out_ref[span, :] = part[depth + last, span, :] + from_y[last, span, :]

        @pl.when(down)
        def _():
            z_arrival(z, q).wait_recv()
            out_ref[span, :] += from_z[z, span, :]

        @pl.when(up)
        def _():
            z_arrival(depth, q).wait_recv()
            out_ref[span, :] += from_z[depth, span, :]

    b_swap.wait_send()

    def finish(s, _):
        a_swap(s).wait_send()
        a_swap(depth + s).wait_send()
        for q in range(CHUNKS):
            y_copy(s, q).wait_send()

            @pl.when(s < last)
            def _():
                z_copy(s, q).wait_send()
        return 0

    lax.fori_loop(0, depth, finish, 0)


def shards(devices, amplitudes, integrals, pair_irrep, column_irrep):
    depth = devices // 4
    local_k, local_m = amplitudes.shape
    width = integrals.shape[1]
    rows = local_m // devices
    scratch = [
        pltpu.VMEM((2 * depth, 2 * local_k, rows), jnp.float32),
        pltpu.VMEM((2 * local_k, width), jnp.float32),
        pltpu.VMEM((2 * local_k, width), jnp.bfloat16),
        pltpu.VMEM((2 * local_k, width), jnp.bfloat16),
        pltpu.VMEM((2 * depth, rows, width), jnp.float32),
        pltpu.VMEM((depth, rows, width), jnp.float32),
        pltpu.VMEM((depth + 1, rows, width), jnp.float32),
        pltpu.SemaphoreType.DMA((2 * depth,)),
        pltpu.SemaphoreType.DMA,
        pltpu.SemaphoreType.DMA((2 * depth,)),
        pltpu.SemaphoreType.DMA((2 * depth,)),
        pltpu.SemaphoreType.DMA,
        pltpu.SemaphoreType.DMA,
        pltpu.SemaphoreType.DMA((depth, CHUNKS)),
        pltpu.SemaphoreType.DMA((depth, CHUNKS)),
        pltpu.SemaphoreType.DMA((depth, CHUNKS)),
        pltpu.SemaphoreType.DMA((depth + 1, CHUNKS)),
    ]
    return pl.pallas_call(
        functools.partial(kernel, depth),
        out_shape=jax.ShapeDtypeStruct((rows, width), jnp.float32),
        in_specs=[
            pl.BlockSpec(memory_space=pl.ANY),
            pl.BlockSpec(memory_space=pl.ANY),
            pl.BlockSpec(memory_space=pltpu.SMEM),
            pl.BlockSpec(memory_space=pltpu.SMEM),
        ],
        out_specs=pl.BlockSpec(memory_space=pltpu.VMEM),
        scratch_shapes=scratch,
        cost_estimate=pl.CostEstimate(
            flops=12 * local_k * local_m * width, bytes_accessed=4 * local_k * (local_m + width), transcendentals=0),
        compiler_params=pltpu.CompilerParams(
            collective_id=0, has_side_effects=True, vmem_limit_bytes=60 * 1024 * 1024),
    )(amplitudes, integrals, pair_irrep, column_irrep)


def solution(mesh):
    placed = (P("row", "groups"), P("row", "groups"), P("groups"), P("groups"))
    return jax.shard_map(
        functools.partial(shards, mesh.shape["row"]), mesh=mesh, in_specs=placed, out_specs=P("row", "groups"),
        check_vma=False)
```

time: 231 us -> 104 us (0.45)
  waiting for transfers between devices: 178 us -> 0 us
  Pallas kernels: 0 us -> 100 us
  matrix products: 31.6 us -> 0 us
  between operations: 13.4 us -> 0.01 us
    reduce_scatter x1 -> x0, waiting for transfers between devices: 178 us -> none  [shards(): lax.psum_scatter(lax.dot_general(amplitudes, masked, (((0,), (0,)), ((),...]
    pallas_call x0 -> x1, Pallas kernels: none -> 100 us  [shards(): pl.pallas_call(functools.partial(kernel, depth), out_shape=jax.ShapeDtype...]
    dot_general x1 -> x0, matrix products: 31.6 us -> none  [shards(): lax.dot_general(amplitudes, masked, (((0,), (0,)), ((), ())), precision=l...]
    reduce_scatter x1 -> x0, local copies, waits for them, and re-layouts: 2.53 us -> none  [shards(): lax.psum_scatter(lax.dot_general(amplitudes, masked, (((0,), (0,)), ((),...]
  transfers between devices with their start and end apart: 1 -> 0, of which waited for: 1 -> 0; matrix products, arithmetic and copies ran while one was open for 0% -> 0% of each run, Pallas kernels for 0% -> 0%
where the time goes in v1:
time: 104 us; the launch traced here: 102 us
  Pallas kernels  100 us (96%)
  local copies, waits for them, and re-layouts  2.26 us (2%)
    pallas_call x1, Pallas kernels, shards(): pl.pallas_call(functools.partial(kernel, depth), out_shape=jax.ShapeDtype...  100 us
    unnamed x1, local copies, waits for them, and re-layouts  2.26 us

profile of v1, /device:TPU:25, one launch (start us, length us, event | category | flops | bytes accessed | tf_op | source)
XLA Modules:
  0.0 102.3 jit_solution(4835943275261294159)
XLA Ops:
  0.0 100.0 %shard_map.46 = f32[512,512]{1,0:T(8,128)} custom-call(f32[384,8192]{1,0:T(8,128)} %a_hbm.1, f32[384,512]{1,0:T(8,128)} %b_hbm.1, s32[96]{0:T(128)} %pair_ref.1, s32[8]{0:T(128)} %column_ref.1), custom_call_target="tpu_custom_call" | custom-call | flops 19327352832 | bytes 13369344 | tf_op jit(solution)/shard_map/pallas_call | solution.py:219
  100.0 2.3 %copy.6 = f32[512,512]{1,0:T(8,128)} copy(f32[512,512]{1,0:T(8,128)} %shard_map.46) | data formatting | bytes 2097152

commit v2 on v1

--- a/solution.py
+++ b/solution.py
@@ -10,6 +10,7 @@
 TILE = 64
 MESH = pl.DeviceIdType.MESH
 CHUNKS = 4
+Z_FIRST = 3
 
 
 def split(x):
@@ -18,11 +19,14 @@
     return high, low
 
 
-def kernel(depth, a_hbm, b_hbm, pair_ref, column_ref, out_ref, a_buf, b_buf, b_high, b_low, part, from_y, from_z,
-           a_sem, b_sem, a_send, a_recv, b_send, b_recv, y_send, y_recv, z_send, z_recv):
+def kernel(depth, a_hbm, b_hbm, pair_ref, column_ref, out_ref, a_buf, b_buf, b_high, b_low, part, from_y, from_z, early_z, early_y,
+           a_sem, b_sem, a_send, a_recv, b_send, b_recv, y_send, y_recv, z_send, z_recv, ez_send, ez_recv, ey_send, ey_recv):
     local_k, width = b_hbm.shape
     rows = out_ref.shape[0]
-    chunk = rows // CHUNKS
+    early = rows * Z_FIRST // 16
+    chunk = (rows - early) // CHUNKS
+    last = depth - 1
+    tail = pl.ds(rows - early, early)
     me = lax.axis_index("row")
     z, y, c = me // 4, (me // 2) % 2, me % 2
     sibling = me + 1 - 2 * c
@@ -48,6 +52,10 @@
         owner = 4 * layer(b % depth) + 2 * side + core
         return pl.ds(pl.multiple_of(owner * rows, rows), rows)
 
+    def slot_of(step):
+        moved = jnp.where(step == 0, 0, jnp.where(step == 1, last, step - 1))
+        return jnp.where(step < depth, moved, step)
+
     def a_local(b):
         return pltpu.make_async_copy(a_hbm.at[:, columns(b, c)], a_buf.at[b, pl.ds(0, local_k)], a_sem.at[b])
 
@@ -70,13 +78,33 @@
     def z_copy(s, q):
         target = layer(s)
         step = jnp.where(target > z, 1, -1)
-        arrives_from_above = (target < z) & (z - 1 == target)
-        slot = jnp.where(arrives_from_above, depth, target)
+        slot = landing(target)
         span = pl.ds(q * chunk, chunk)
         return pltpu.make_async_remote_copy(
             src_ref=part.at[depth + s, span], dst_ref=from_z.at[slot, span], send_sem=z_send.at[s, q],
             recv_sem=z_recv.at[slot, q], device_id={"row": me + 4 * step}, device_id_type=MESH)
 
+    def landing(target):
+        arrives_from_above = (target < z) & (z - 1 == target)
+        return jnp.where(arrives_from_above, depth, target)
+
+    def early_z_copy(side, s):
+        target = layer(s)
+        step = jnp.where(target > z, 1, -1)
+        slot = side * (depth + 1) + landing(target)
+        return pltpu.make_async_remote_copy(
+            src_ref=part.at[side * depth + s, tail], dst_ref=early_z.at[slot], send_sem=ez_send.at[side * depth + s],
+            recv_sem=ez_recv.at[slot], device_id={"row": me + 4 * step}, device_id_type=MESH)
+
+    def early_z_arrival(slot):
+        return pltpu.make_async_remote_copy(
+            src_ref=early_z.at[slot], dst_ref=early_z.at[slot], send_sem=ez_send.at[0],
+            recv_sem=ez_recv.at[slot], device_id={"row": across}, device_id_type=MESH)
+
+    early_y_copy = pltpu.make_async_remote_copy(
+        src_ref=part.at[last, tail], dst_ref=early_y, send_sem=ey_send, recv_sem=ey_recv,
+        device_id={"row": across}, device_id_type=MESH)
+
     def z_arrival(slot, q):
         span = pl.ds(q * chunk, chunk)
         return pltpu.make_async_remote_copy(
@@ -84,8 +112,8 @@
             recv_sem=z_recv.at[slot, q], device_id={"row": across}, device_id_type=MESH)
 
     b_local.start()
-    for b in range(2 * depth):
-        a_local(b).start()
+    for step in range(2 * depth):
+        a_local(slot_of(step)).start()
 
     barrier = pltpu.get_barrier_semaphore()
     pl.semaphore_signal(barrier, inc=1, device_id={"row": sibling}, device_id_type=MESH)
@@ -102,8 +130,8 @@
     pl.semaphore_wait(barrier, 2 + jnp.where(up, 1, 0) + jnp.where(down, 1, 0))
 
     b_swap.start()
-    for b in range(2 * depth):
-        a_swap(b).start()
+    for step in range(2 * depth):
+        a_swap(slot_of(step)).start()
 
     block_of = lax.broadcasted_iota(jnp.int32, (TILE, width), 1) // TILE
     labels = jnp.zeros((TILE, width), jnp.int32)
@@ -125,7 +153,12 @@
 
     half = rows // 2
 
-    def multiply(b, _):
+    def is_fed(s):
+        target = layer(s)
+        return ((target > z) & down) | ((target < z) & up)
+
+    def multiply(step, _):
+        b = slot_of(step)
         a_local(b).wait()
         a_swap(b).wait_recv()
         for t in range(2):
@@ -134,17 +167,35 @@
             part[b, pl.ds(t * half, half), :] = (
                 dot(high, b_high[...]) + dot(high, b_low[...]) + dot(low, b_high[...]))
 
-            @pl.when(b < depth)
+            @pl.when(step < depth)
             def _():
                 for q in range(t * CHUNKS // 2, (t + 1) * CHUNKS // 2):
                     y_copy(b, q).start()
+
+        side, s = b // depth, b % depth
+
+        @pl.when((s < last) & jnp.logical_not(is_fed(s)))
+        def _():
+            early_z_copy(side, s).start()
         return 0
 
     lax.fori_loop(0, 2 * depth, multiply, 0)
 
+    def early_forward(s, _):
+        @pl.when(is_fed(s))
+        def _():
+            for side in range(2):
+                slot = side * (depth + 1) + layer(s)
+                early_z_arrival(slot).wait_recv()
+                part[side * depth + s, tail, :] += early_z[slot]
+                early_z_copy(side, s).start()
+        return 0
+
+    lax.fori_loop(0, last, early_forward, 0)
+
     def forward(s, _):
+        fed = is_fed(s)
         target = layer(s)
-        fed = ((target > z) & down) | ((target < z) & up)
         for q in range(CHUNKS):
             span = pl.ds(q * chunk, chunk)
             y_copy(s, q).wait_recv()
@@ -158,9 +209,26 @@
             z_copy(s, q).start()
         return 0
 
-    lax.fori_loop(0, depth - 1, forward, 0)
-
-    last = depth - 1
+    forward(0, 0)
+
+    for side in range(2):
+        @pl.when(down)
+        def _():
+            slot = side * (depth + 1) + z
+            early_z_arrival(slot).wait_recv()
+            part[side * depth + last, tail, :] += early_z[slot]
+
+        @pl.when(up)
+        def _():
+            slot = side * (depth + 1) + depth
+            early_z_arrival(slot).wait_recv()
+            part[side * depth + last, tail, :] += early_z[slot]
+
+        if side == 0:
+            early_y_copy.start()
+
+    lax.fori_loop(1, last, forward, 0)
+
     for q in range(CHUNKS):
         span = pl.ds(q * chunk, chunk)
         y_copy(last, q).wait_recv()
@@ -176,6 +244,9 @@
             z_arrival(depth, q).wait_recv()
             out_ref[span, :] += from_z[depth, span, :]
 
+    early_y_copy.wait_recv()
+    out_ref[tail, :] = part[depth + last, tail, :] + early_y[...]
+    early_y_copy.wait_send()
     b_swap.wait_send()
 
     def finish(s, _):
@@ -187,6 +258,11 @@
             @pl.when(s < last)
             def _():
                 z_copy(s, q).wait_send()
+
+        @pl.when(s < last)
+        def _():
+            early_z_copy(0, s).wait_send()
+            early_z_copy(1, s).wait_send()
         return 0
 
     lax.fori_loop(0, depth, finish, 0)
@@ -197,6 +273,7 @@
     local_k, local_m = amplitudes.shape
     width = integrals.shape[1]
     rows = local_m // devices
+    early = rows * Z_FIRST // 16
     scratch = [
         pltpu.VMEM((2 * depth, 2 * local_k, rows), jnp.float32),
         pltpu.VMEM((2 * local_k, width), jnp.float32),
@@ -205,6 +282,8 @@
         pltpu.VMEM((2 * depth, rows, width), jnp.float32),
         pltpu.VMEM((depth, rows, width), jnp.float32),
         pltpu.VMEM((depth + 1, rows, width), jnp.float32),
+        pltpu.VMEM((2 * (depth + 1), early, width), jnp.float32),
+        pltpu.VMEM((early, width), jnp.float32),
         pltpu.SemaphoreType.DMA((2 * depth,)),
         pltpu.SemaphoreType.DMA,
         pltpu.SemaphoreType.DMA((2 * depth,)),
@@ -215,6 +294,10 @@
         pltpu.SemaphoreType.DMA((depth, CHUNKS)),
         pltpu.SemaphoreType.DMA((depth, CHUNKS)),
         pltpu.SemaphoreType.DMA((depth + 1, CHUNKS)),
+        pltpu.SemaphoreType.DMA((2 * depth,)),
+        pltpu.SemaphoreType.DMA((2 * (depth + 1),)),
+        pltpu.SemaphoreType.DMA,
+        pltpu.SemaphoreType.DMA,
     ]
     return pl.pallas_call(
         functools.partial(kernel, depth),

time: 104 us -> 96.3 us (0.926); the launches traced: 102 us -> 96.2 us
  Pallas kernels: 100 us -> 93.9 us
    pallas_call x1, Pallas kernels: 100 us -> 93.9 us  [shards(): pl.pallas_call(functools.partial(kernel, depth), out_shape=jax.ShapeDtype...]
where the time goes in v2:
time: 96.3 us; the launch traced here: 96.2 us
  Pallas kernels  93.9 us (98%)
  local copies, waits for them, and re-layouts  2.26 us (2%)
    pallas_call x1, Pallas kernels, shards(): pl.pallas_call(functools.partial(kernel, depth), out_shape=jax.ShapeDtype...  93.9 us
    unnamed x1, local copies, waits for them, and re-layouts  2.26 us

profile of v2, /device:TPU:25, one launch (start us, length us, event | category | flops | bytes accessed | tf_op | source)
XLA Modules:
  0.0 96.2 jit_solution(8611087065731799138)
XLA Ops:
  0.0 93.9 %shard_map.46 = f32[512,512]{1,0:T(8,128)} custom-call(f32[384,8192]{1,0:T(8,128)} %a_hbm.1, f32[384,512]{1,0:T(8,128)} %b_hbm.1, s32[96]{0:T(128)} %pair_ref.1, s32[8]{0:T(128)} %column_ref.1), custom_call_target="tpu_custom_call" | custom-call | flops 19327352832 | bytes 13369344 | tf_op jit(solution)/shard_map/pallas_call | solution.py:302
  93.9 2.3 %copy.6 = f32[512,512]{1,0:T(8,128)} copy(f32[512,512]{1,0:T(8,128)} %shard_map.46) | data formatting | bytes 2097152

commit v3 on v2

--- a/solution.py
+++ b/solution.py
@@ -9,8 +9,10 @@
 
 TILE = 64
 MESH = pl.DeviceIdType.MESH
-CHUNKS = 4
-Z_FIRST = 3
+BOUNDS = (10, 20, 32, 44, 56, 64)
+CHUNKS = len(BOUNDS) - 1
+OWN_AT = 3
+AHEAD = 1
 
 
 def split(x):
@@ -23,10 +25,11 @@
            a_sem, b_sem, a_send, a_recv, b_send, b_recv, y_send, y_recv, z_send, z_recv, ez_send, ez_recv, ey_send, ey_recv):
     local_k, width = b_hbm.shape
     rows = out_ref.shape[0]
-    early = rows * Z_FIRST // 16
-    chunk = (rows - early) // CHUNKS
+    bounds = [rows * bound // 64 for bound in BOUNDS]
+    spans = [pl.ds(start, end - start) for start, end in zip(bounds, bounds[1:])]
+    head = pl.ds(0, bounds[0])
+    half = rows // 2
     last = depth - 1
-    tail = pl.ds(rows - early, early)
     me = lax.axis_index("row")
     z, y, c = me // 4, (me // 2) % 2, me % 2
     sibling = me + 1 - 2 * c
@@ -46,23 +49,24 @@
             found = jnp.where(s == k, order[k], found)
         return found
 
-    def columns(b, core):
+    def columns(b, core, t):
         other = 1 - b // depth
         side = y + other * (1 - 2 * y)
         owner = 4 * layer(b % depth) + 2 * side + core
-        return pl.ds(pl.multiple_of(owner * rows, rows), rows)
+        return pl.ds(pl.multiple_of(owner * rows + t * half, half), half)
 
     def slot_of(step):
-        moved = jnp.where(step == 0, 0, jnp.where(step == 1, last, step - 1))
+        moved = jnp.where(step < OWN_AT, step, jnp.where(step == OWN_AT, last, step - 1))
         return jnp.where(step < depth, moved, step)
 
-    def a_local(b):
-        return pltpu.make_async_copy(a_hbm.at[:, columns(b, c)], a_buf.at[b, pl.ds(0, local_k)], a_sem.at[b])
-
-    def a_swap(b):
-        return pltpu.make_async_remote_copy(
-            src_ref=a_hbm.at[:, columns(b, 1 - c)], dst_ref=a_buf.at[b, pl.ds(local_k, local_k)],
-            send_sem=a_send.at[b], recv_sem=a_recv.at[b], device_id={"row": sibling}, device_id_type=MESH)
+    def a_local(b, t):
+        return pltpu.make_async_copy(
+            a_hbm.at[:, columns(b, c, t)], a_buf.at[b, t, pl.ds(0, local_k)], a_sem.at[b, t])
+
+    def a_swap(b, t):
+        return pltpu.make_async_remote_copy(
+            src_ref=a_hbm.at[:, columns(b, 1 - c, t)], dst_ref=a_buf.at[b, t, pl.ds(local_k, local_k)],
+            send_sem=a_send.at[b, t], recv_sem=a_recv.at[b, t], device_id={"row": sibling}, device_id_type=MESH)
 
     b_local = pltpu.make_async_copy(b_hbm, b_buf.at[pl.ds(0, local_k)], b_sem)
     b_swap = pltpu.make_async_remote_copy(
@@ -70,7 +74,7 @@
         device_id={"row": sibling}, device_id_type=MESH)
 
     def y_copy(s, q):
-        span = pl.ds(q * chunk, chunk)
+        span = spans[q]
         return pltpu.make_async_remote_copy(
             src_ref=part.at[s, span], dst_ref=from_y.at[s, span], send_sem=y_send.at[s, q], recv_sem=y_recv.at[s, q],
             device_id={"row": across}, device_id_type=MESH)
@@ -79,7 +83,7 @@
         target = layer(s)
         step = jnp.where(target > z, 1, -1)
         slot = landing(target)
-        span = pl.ds(q * chunk, chunk)
+        span = spans[q]
         return pltpu.make_async_remote_copy(
             src_ref=part.at[depth + s, span], dst_ref=from_z.at[slot, span], send_sem=z_send.at[s, q],
             recv_sem=z_recv.at[slot, q], device_id={"row": me + 4 * step}, device_id_type=MESH)
@@ -93,7 +97,7 @@
         step = jnp.where(target > z, 1, -1)
         slot = side * (depth + 1) + landing(target)
         return pltpu.make_async_remote_copy(
-            src_ref=part.at[side * depth + s, tail], dst_ref=early_z.at[slot], send_sem=ez_send.at[side * depth + s],
+            src_ref=part.at[side * depth + s, head], dst_ref=early_z.at[slot], send_sem=ez_send.at[side * depth + s],
             recv_sem=ez_recv.at[slot], device_id={"row": me + 4 * step}, device_id_type=MESH)
 
     def early_z_arrival(slot):
@@ -102,18 +106,19 @@
             recv_sem=ez_recv.at[slot], device_id={"row": across}, device_id_type=MESH)
 
     early_y_copy = pltpu.make_async_remote_copy(
-        src_ref=part.at[last, tail], dst_ref=early_y, send_sem=ey_send, recv_sem=ey_recv,
+        src_ref=part.at[last, head], dst_ref=early_y, send_sem=ey_send, recv_sem=ey_recv,
         device_id={"row": across}, device_id_type=MESH)
 
     def z_arrival(slot, q):
-        span = pl.ds(q * chunk, chunk)
+        span = spans[q]
         return pltpu.make_async_remote_copy(
             src_ref=from_z.at[slot, span], dst_ref=from_z.at[slot, span], send_sem=z_send.at[0, q],
             recv_sem=z_recv.at[slot, q], device_id={"row": across}, device_id_type=MESH)
 
     b_local.start()
     for step in range(2 * depth):
-        a_local(slot_of(step)).start()
+        for t in range(2):
+            a_local(slot_of(step), t).start()
 
     barrier = pltpu.get_barrier_semaphore()
     pl.semaphore_signal(barrier, inc=1, device_id={"row": sibling}, device_id_type=MESH)
@@ -130,8 +135,9 @@
     pl.semaphore_wait(barrier, 2 + jnp.where(up, 1, 0) + jnp.where(down, 1, 0))
 
     b_swap.start()
-    for step in range(2 * depth):
-        a_swap(slot_of(step)).start()
+    for step in range(AHEAD):
+        for t in range(2):
+            a_swap(slot_of(step), t).start()
 
     block_of = lax.broadcasted_iota(jnp.int32, (TILE, width), 1) // TILE
     labels = jnp.zeros((TILE, width), jnp.int32)
@@ -151,32 +157,38 @@
     for i in range(local_k // TILE):
         mask(i, sibling, local_k)
 
-    half = rows // 2
-
     def is_fed(s):
         target = layer(s)
         return ((target > z) & down) | ((target < z) & up)
 
     def multiply(step, _):
         b = slot_of(step)
-        a_local(b).wait()
-        a_swap(b).wait_recv()
+
+        @pl.when(step < 2 * depth - AHEAD)
+        def _():
+            for t in range(2):
+                a_swap(slot_of(step + AHEAD), t).start()
+
+        side, s = b // depth, b % depth
         for t in range(2):
-            high, low = split(a_buf[b, :, pl.ds(t * half, half)].T)
+            a_local(b, t).wait()
+            a_swap(b, t).wait_recv()
+            high, low = split(a_buf[b, t].T)
             dot = functools.partial(jnp.dot, preferred_element_type=jnp.float32)
             part[b, pl.ds(t * half, half), :] = (
                 dot(high, b_high[...]) + dot(high, b_low[...]) + dot(low, b_high[...]))
 
+            if t == 0:
+                @pl.when((s < last) & jnp.logical_not(is_fed(s)))
+                def _():
+                    early_z_copy(side, s).start()
+
             @pl.when(step < depth)
             def _():
-                for q in range(t * CHUNKS // 2, (t + 1) * CHUNKS // 2):
-                    y_copy(b, q).start()
-
-        side, s = b // depth, b % depth
-
-        @pl.when((s < last) & jnp.logical_not(is_fed(s)))
-        def _():
-            early_z_copy(side, s).start()
+                for q in range(CHUNKS):
+                    if bounds[q + 1] <= half * (t + 1) and bounds[q + 1] > half * t:
+                        y_copy(b, q).start()
+
         return 0
 
     lax.fori_loop(0, 2 * depth, multiply, 0)
@@ -187,7 +199,7 @@
             for side in range(2):
                 slot = side * (depth + 1) + layer(s)
                 early_z_arrival(slot).wait_recv()
-                part[side * depth + s, tail, :] += early_z[slot]
+                part[side * depth + s, head, :] += early_z[slot]
                 early_z_copy(side, s).start()
         return 0
 
@@ -197,7 +209,7 @@
         fed = is_fed(s)
         target = layer(s)
         for q in range(CHUNKS):
-            span = pl.ds(q * chunk, chunk)
+            span = spans[q]
             y_copy(s, q).wait_recv()
             part[depth + s, span, :] += from_y[s, span, :]
 
@@ -216,13 +228,13 @@
         def _():
             slot = side * (depth + 1) + z
             early_z_arrival(slot).wait_recv()
-            part[side * depth + last, tail, :] += early_z[slot]
+            part[side * depth + last, head, :] += early_z[slot]
 
         @pl.when(up)
         def _():
             slot = side * (depth + 1) + depth
             early_z_arrival(slot).wait_recv()
-            part[side * depth + last, tail, :] += early_z[slot]
+            part[side * depth + last, head, :] += early_z[slot]
 
         if side == 0:
             early_y_copy.start()
@@ -230,7 +242,7 @@
     lax.fori_loop(1, last, forward, 0)
 
     for q in range(CHUNKS):
-        span = pl.ds(q * chunk, chunk)
+        span = spans[q]
         y_copy(last, q).wait_recv()
         out_ref[span, :] = part[depth + last, span, :] + from_y[last, span, :]
 
@@ -245,13 +257,14 @@
             out_ref[span, :] += from_z[depth, span, :]
 
     early_y_copy.wait_recv()
-    out_ref[tail, :] = part[depth + last, tail, :] + early_y[...]
+    out_ref[head, :] = part[depth + last, head, :] + early_y[...]
     early_y_copy.wait_send()
     b_swap.wait_send()
 
     def finish(s, _):
-        a_swap(s).wait_send()
-        a_swap(depth + s).wait_send()
+        for t in range(2):
+            a_swap(s, t).wait_send()
+            a_swap(depth + s, t).wait_send()
         for q in range(CHUNKS):
             y_copy(s, q).wait_send()
 
@@ -273,9 +286,9 @@
     local_k, local_m = amplitudes.shape
     width = integrals.shape[1]
     rows = local_m // devices
-    early = rows * Z_FIRST // 16
+    early = rows * BOUNDS[0] // 64
     scratch = [
-        pltpu.VMEM((2 * depth, 2 * local_k, rows), jnp.float32),
+        pltpu.VMEM((2 * depth, 2, 2 * local_k, rows // 2), jnp.float32),
         pltpu.VMEM((2 * local_k, width), jnp.float32),
         pltpu.VMEM((2 * local_k, width), jnp.bfloat16),
         pltpu.VMEM((2 * local_k, width), jnp.bfloat16),
@@ -284,10 +297,10 @@
         pltpu.VMEM((depth + 1, rows, width), jnp.float32),
         pltpu.VMEM((2 * (depth + 1), early, width), jnp.float32),
         pltpu.VMEM((early, width), jnp.float32),
-        pltpu.SemaphoreType.DMA((2 * depth,)),
-        pltpu.SemaphoreType.DMA,
-        pltpu.SemaphoreType.DMA((2 * depth,)),
-        pltpu.SemaphoreType.DMA((2 * depth,)),
+        pltpu.SemaphoreType.DMA((2 * depth, 2)),
+        pltpu.SemaphoreType.DMA,
+        pltpu.SemaphoreType.DMA((2 * depth, 2)),
+        pltpu.SemaphoreType.DMA((2 * depth, 2)),
         pltpu.SemaphoreType.DMA,
         pltpu.SemaphoreType.DMA,
         pltpu.SemaphoreType.DMA((depth, CHUNKS)),
@@ -301,7 +314,7 @@
     ]
     return pl.pallas_call(
         functools.partial(kernel, depth),
-        out_shape=jax.ShapeDtypeStruct((rows, width), jnp.float32),
+        out_shape=pltpu.VMEM((rows, width), jnp.float32),
         in_specs=[
             pl.BlockSpec(memory_space=pl.ANY),
             pl.BlockSpec(memory_space=pl.ANY),

time: 96.3 us -> 91.5 us (0.950)
  Pallas kernels: 93.9 us -> 89.8 us
  local copies, waits for them, and re-layouts: 2.26 us -> 0.97 us
    pallas_call x1, Pallas kernels: 93.9 us -> 89.8 us  [shards(): pl.pallas_call(functools.partial(kernel, depth), out_shape=pltpu.VMEM((ro...]
    unnamed x1, local copies, waits for them, and re-layouts: 2.26 us -> 0.97 us
where the time goes in v3:
time: 91.5 us; the launch traced here: 90.8 us
  Pallas kernels  89.8 us (98%)
  local copies, waits for them, and re-layouts  0.97 us (1%)
    pallas_call x1, Pallas kernels, shards(): pl.pallas_call(functools.partial(kernel, depth), out_shape=pltpu.VMEM((ro...  89.8 us

profile of v3, /device:TPU:25, one launch (start us, length us, event | category | flops | bytes accessed | tf_op | source)
XLA Modules:
  0.0 90.8 jit_solution(10151657420363208992)
XLA Ops:
  0.0 89.8 %shard_map.46 = f32[512,512]{1,0:T(8,128)S(1)} custom-call(f32[384,8192]{1,0:T(8,128)} %a_hbm.1, f32[384,512]{1,0:T(8,128)} %b_hbm.1, s32[96]{0:T(128)} %pair_ref.1, s32[8]{0:T(128)} %column_ref.1), custom_call_target="tpu_custom_call" | custom-call | flops 19327352832 | bytes 13369344 | tf_op jit(solution)/shard_map/pallas_call | solution.py:315
  89.8 1.0 %copy.6 = f32[512,512]{1,0:T(8,128)} copy(f32[512,512]{1,0:T(8,128)S(1)} %shard_map.46) | data formatting | bytes 2097152

commit v4 on v3

--- a/solution.py
+++ b/solution.py
@@ -9,10 +9,9 @@
 
 TILE = 64
 MESH = pl.DeviceIdType.MESH
-BOUNDS = (10, 20, 32, 44, 56, 64)
+BOUNDS = (11, 20, 32, 44, 56, 64)
 CHUNKS = len(BOUNDS) - 1
 OWN_AT = 3
-AHEAD = 1
 
 
 def split(x):
@@ -22,7 +21,9 @@
 
 
 def kernel(depth, a_hbm, b_hbm, pair_ref, column_ref, out_ref, a_buf, b_buf, b_high, b_low, part, from_y, from_z, early_z, early_y,
-           a_sem, b_sem, a_send, a_recv, b_send, b_recv, y_send, y_recv, z_send, z_recv, ez_send, ez_recv, ey_send, ey_recv):
+           a_cross, cross_out, cross_in,
+           a_sem, b_sem, a_send, a_recv, b_send, b_recv, y_send, y_recv, z_send, z_recv, ez_send, ez_recv, ey_send, ey_recv,
+           ac_sem, c_send, c_recv):
     local_k, width = b_hbm.shape
     rows = out_ref.shape[0]
     bounds = [rows * bound // 64 for bound in BOUNDS]
@@ -68,6 +69,16 @@
             src_ref=a_hbm.at[:, columns(b, 1 - c, t)], dst_ref=a_buf.at[b, t, pl.ds(local_k, local_k)],
             send_sem=a_send.at[b, t], recv_sem=a_recv.at[b, t], device_id={"row": sibling}, device_id_type=MESH)
 
+    pieces = [(start, end) for start, end in zip([0] + bounds, bounds) if end <= half]
+    a_other = pltpu.make_async_copy(a_hbm.at[:, columns(0, 1 - c, 0)], a_cross, ac_sem)
+
+    def cross(p):
+        start, end = pieces[p]
+        span = pl.ds(start, end - start)
+        return pltpu.make_async_remote_copy(
+            src_ref=cross_out.at[span], dst_ref=cross_in.at[span], send_sem=c_send.at[p], recv_sem=c_recv.at[p],
+            device_id={"row": sibling}, device_id_type=MESH)
+
     b_local = pltpu.make_async_copy(b_hbm, b_buf.at[pl.ds(0, local_k)], b_sem)
     b_swap = pltpu.make_async_remote_copy(
         src_ref=b_hbm, dst_ref=b_buf.at[pl.ds(local_k, local_k)], send_sem=b_send, recv_sem=b_recv,
@@ -115,11 +126,6 @@
             src_ref=from_z.at[slot, span], dst_ref=from_z.at[slot, span], send_sem=z_send.at[0, q],
             recv_sem=z_recv.at[slot, q], device_id={"row": across}, device_id_type=MESH)
 
-    b_local.start()
-    for step in range(2 * depth):
-        for t in range(2):
-            a_local(slot_of(step), t).start()
-
     barrier = pltpu.get_barrier_semaphore()
     pl.semaphore_signal(barrier, inc=1, device_id={"row": sibling}, device_id_type=MESH)
     pl.semaphore_signal(barrier, inc=1, device_id={"row": across}, device_id_type=MESH)
@@ -132,13 +138,10 @@
     def _():
         pl.semaphore_signal(barrier, inc=1, device_id={"row": me - 4}, device_id_type=MESH)
 
-    pl.semaphore_wait(barrier, 2 + jnp.where(up, 1, 0) + jnp.where(down, 1, 0))
-
-    b_swap.start()
-    for step in range(AHEAD):
-        for t in range(2):
-            a_swap(slot_of(step), t).start()
-
+    b_local.start()
+    a_other.start()
+    a_local(0, 0).start()
+    a_local(0, 1).start()
     block_of = lax.broadcasted_iota(jnp.int32, (TILE, width), 1) // TILE
     labels = jnp.zeros((TILE, width), jnp.int32)
     for j in range(width // TILE):
@@ -153,45 +156,79 @@
     b_local.wait()
     for i in range(local_k // TILE):
         mask(i, me, 0)
+    def product(x, span):
+        high, low = split(x.T)
+        dot = functools.partial(jnp.dot, preferred_element_type=jnp.float32)
+        return dot(high, b_high[span, :]) + dot(high, b_low[span, :]) + dot(low, b_high[span, :])
+
+    own, both = pl.ds(0, local_k), pl.ds(0, 2 * local_k)
+    a_other.wait()
+    cross_out[...] = product(a_cross[...], own)
+
+    pl.semaphore_wait(barrier, 2 + jnp.where(up, 1, 0) + jnp.where(down, 1, 0))
+
+    for p in range(len(pieces)):
+        cross(p).start()
+    b_swap.start()
+    a_swap(0, 1).start()
+    for step in range(1, 2 * depth):
+        for t in range(2):
+            a_local(slot_of(step), t).start()
+
+    def is_fed(s):
+        target = layer(s)
+        return ((target > z) & down) | ((target < z) & up)
+
+    a_local(0, 0).wait()
+    part[0, pl.ds(0, half), :] = product(a_buf[0, 0, own, :], own)
+    for p, (start, end) in enumerate(pieces):
+        span = pl.ds(start, end - start)
+        cross(p).wait_recv()
+        part[0, span, :] += cross_in[span, :]
+        if p == 0:
+            @pl.when(jnp.logical_not(is_fed(0)))
+            def _():
+                early_z_copy(0, 0).start()
+        else:
+            y_copy(0, p - 1).start()
+
     b_swap.wait_recv()
     for i in range(local_k // TILE):
         mask(i, sibling, local_k)
 
-    def is_fed(s):
-        target = layer(s)
-        return ((target > z) & down) | ((target < z) & up)
+    def tile(step, b, t):
+        side, s = b // depth, b % depth
+        a_local(b, t).wait()
+        a_swap(b, t).wait_recv()
+        part[b, pl.ds(t * half, half), :] = product(a_buf[b, t], both)
+
+        if t == 0:
+            @pl.when((s < last) & jnp.logical_not(is_fed(s)))
+            def _():
+                early_z_copy(side, s).start()
+
+        @pl.when(step < depth)
+        def _():
+            for q in range(CHUNKS):
+                if half * t < bounds[q + 1] <= half * (t + 1):
+                    y_copy(b, q).start()
+
+    def swap_next(step):
+        for t in range(2):
+            a_swap(slot_of(step + 1), t).start()
 
     def multiply(step, _):
-        b = slot_of(step)
-
-        @pl.when(step < 2 * depth - AHEAD)
-        def _():
-            for t in range(2):
-                a_swap(slot_of(step + AHEAD), t).start()
-
-        side, s = b // depth, b % depth
+        @pl.when(step < 2 * depth - 1)
+        def _():
+            swap_next(step)
+
         for t in range(2):
-            a_local(b, t).wait()
-            a_swap(b, t).wait_recv()
-            high, low = split(a_buf[b, t].T)
-            dot = functools.partial(jnp.dot, preferred_element_type=jnp.float32)
-            part[b, pl.ds(t * half, half), :] = (
-                dot(high, b_high[...]) + dot(high, b_low[...]) + dot(low, b_high[...]))
-
-            if t == 0:
-                @pl.when((s < last) & jnp.logical_not(is_fed(s)))
-                def _():
-                    early_z_copy(side, s).start()
-
-            @pl.when(step < depth)
-            def _():
-                for q in range(CHUNKS):
-                    if bounds[q + 1] <= half * (t + 1) and bounds[q + 1] > half * t:
-                        y_copy(b, q).start()
-
+            tile(step, slot_of(step), t)
         return 0
 
-    lax.fori_loop(0, 2 * depth, multiply, 0)
+    swap_next(0)
+    tile(0, 0, 1)
+    lax.fori_loop(1, 2 * depth, multiply, 0)
 
     def early_forward(s, _):
         @pl.when(is_fed(s))
@@ -259,11 +296,17 @@
     early_y_copy.wait_recv()
     out_ref[head, :] = part[depth + last, head, :] + early_y[...]
     early_y_copy.wait_send()
+    for p in range(len(pieces)):
+        cross(p).wait_send()
     b_swap.wait_send()
 
     def finish(s, _):
+        @pl.when(s > 0)
+        def _():
+            a_swap(s, 0).wait_send()
+
+        a_swap(s, 1).wait_send()
         for t in range(2):
-            a_swap(s, t).wait_send()
             a_swap(depth + s, t).wait_send()
         for q in range(CHUNKS):
             y_copy(s, q).wait_send()
@@ -297,6 +340,9 @@
         pltpu.VMEM((depth + 1, rows, width), jnp.float32),
         pltpu.VMEM((2 * (depth + 1), early, width), jnp.float32),
         pltpu.VMEM((early, width), jnp.float32),
+        pltpu.VMEM((local_k, rows // 2), jnp.float32),
+        pltpu.VMEM((rows // 2, width), jnp.float32),
+        pltpu.VMEM((rows // 2, width), jnp.float32),
         pltpu.SemaphoreType.DMA((2 * depth, 2)),
         pltpu.SemaphoreType.DMA,
         pltpu.SemaphoreType.DMA((2 * depth, 2)),
@@ -311,6 +357,9 @@
         pltpu.SemaphoreType.DMA((2 * (depth + 1),)),
         pltpu.SemaphoreType.DMA,
         pltpu.SemaphoreType.DMA,
+        pltpu.SemaphoreType.DMA,
+        pltpu.SemaphoreType.DMA((CHUNKS,)),
+        pltpu.SemaphoreType.DMA((CHUNKS,)),
     ]
     return pl.pallas_call(
         functools.partial(kernel, depth),

time: 91.5 us -> 89.5 us (0.978)
  Pallas kernels: 89.8 us -> 87.2 us
    pallas_call x1, Pallas kernels: 89.8 us -> 87.2 us  [shards(): pl.pallas_call(functools.partial(kernel, depth), out_shape=pltpu.VMEM((ro...]
where the time goes in v4:
time: 89.5 us; the launch traced here: 88.1 us
  Pallas kernels  87.2 us (97%)
  local copies, waits for them, and re-layouts  0.97 us (1%)
    pallas_call x1, Pallas kernels, shards(): pl.pallas_call(functools.partial(kernel, depth), out_shape=pltpu.VMEM((ro...  87.2 us

profile of v4, /device:TPU:25, one launch (start us, length us, event | category | flops | bytes accessed | tf_op | source)
XLA Modules:
  0.0 88.1 jit_solution(2017619574887638399)
XLA Ops:
  0.0 87.2 %shard_map.46 = f32[512,512]{1,0:T(8,128)S(1)} custom-call(f32[384,8192]{1,0:T(8,128)} %a_hbm.1, f32[384,512]{1,0:T(8,128)} %b_hbm.1, s32[96]{0:T(128)} %pair_ref.1, s32[8]{0:T(128)} %column_ref.1), custom_call_target="tpu_custom_call" | custom-call | flops 19327352832 | bytes 13369344 | tf_op jit(solution)/shard_map/pallas_call | solution.py:364
  87.2 1.0 %copy.6 = f32[512,512]{1,0:T(8,128)} copy(f32[512,512]{1,0:T(8,128)S(1)} %shard_map.46) | data formatting | bytes 2097152

commit v5 on v4

--- a/solution.py
+++ b/solution.py
@@ -258,7 +258,7 @@
             z_copy(s, q).start()
         return 0
 
-    forward(0, 0)
+    lax.fori_loop(0, 2, forward, 0)
 
     for side in range(2):
         @pl.when(down)
@@ -276,7 +276,7 @@
         if side == 0:
             early_y_copy.start()
 
-    lax.fori_loop(1, last, forward, 0)
+    lax.fori_loop(2, last, forward, 0)
 
     for q in range(CHUNKS):
         span = spans[q]

time: 89.5 us -> 89.5 us (level)
  no operation moved by 1% of the time
where the time goes in v5:
time: 89.5 us; the launch traced here: 88.1 us
  Pallas kernels  87.2 us (97%)
  local copies, waits for them, and re-layouts  0.97 us (1%)
    pallas_call x1, Pallas kernels, shards(): pl.pallas_call(functools.partial(kernel, depth), out_shape=pltpu.VMEM((ro...  87.2 us

profile of v5, /device:TPU:25, one launch (start us, length us, event | category | flops | bytes accessed | tf_op | source)
XLA Modules:
  0.0 88.1 jit_solution(6555609887545772869)
XLA Ops:
  0.0 87.2 %shard_map.46 = f32[512,512]{1,0:T(8,128)S(1)} custom-call(f32[384,8192]{1,0:T(8,128)} %a_hbm.1, f32[384,512]{1,0:T(8,128)} %b_hbm.1, s32[96]{0:T(128)} %pair_ref.1, s32[8]{0:T(128)} %column_ref.1), custom_call_target="tpu_custom_call" | custom-call | flops 19327352832 | bytes 13369344 | tf_op jit(solution)/shard_map/pallas_call | solution.py:364
  87.2 1.0 %copy.6 = f32[512,512]{1,0:T(8,128)} copy(f32[512,512]{1,0:T(8,128)S(1)} %shard_map.46) | data formatting | bytes 2097152
